TPU v7x, 32 devices: a whole 2x2x4 slice. The times are simulated.
32 devices in a mesh: groups: 2 (over x), row: 16 (over z, y, core).
Axes of the slice: x: 2, y: 2, z: 4, core: 2. Of those that a mesh axis runs over, the one named last changes fastest.
Arguments:
- basis: float32 [8192, 128], P(('groups', 'row')), parts along dimension 0, may hold values from -6 to 6
- springs: float32 [8192], P(('groups', 'row')), parts along dimension 0, may hold values from 0.25 to 8
- tangent_blocks: float32 [4096, 4096], P(('groups', 'row')), parts along dimension 0, may hold values from -0.375 to 0.375
- tile_rows: int32 [4096], P(('groups', 'row')), parts along dimension 0, may hold values from 0 to 3
- tile_owner: int32 [4096, 1], P(('groups', 'row')), parts along dimension 0, may hold values from 0 to 15, as said below
- tile_offset: int32 [4096], P(('groups', 'row')), parts along dimension 0, may hold values from 0 to 3
- tile_count: int32 [32], P(('groups', 'row')), parts along dimension 0, may hold values from 32 to 128, as said below
Outputs:
- stiff_image: float32 [8192, 128], P(('groups', 'row')), parts along dimension 0
- reduced: float32 [256, 128], P('groups'), parts along dimension 0
There are 2 independent parts, one for each index of `groups`. A program takes and returns all parts, laid end to end along the dimension named above; each array names one. Nothing has to cross between parts.
Inputs may be any that keep to these rules, and one draw needn't show every extreme that they name: The first tile_count[d] slots of device d are live; some device has exactly 128. `tile_owner`: the slab is closed into a shell: every slot of device d names owner (d + o) mod 16 with o one of 0, 1, -1, 4, -4, 5, -5, 8. Among the slots of one device no owner appears more than 32 times, and owner d itself appears exactly 32 times in every device.
All inputs are finite; a program needn't handle non-finite values.
Results may differ from a plain program's by a relative error of at most 0.0003.
Values sent between devices are 32-bit elements; how exact they have to be, the bound alone decides.
A program may use at most 128 MiB of HBM per device.

v0:
```python
import jax
import jax.numpy as jnp
from jax import lax
from jax.sharding import PartitionSpec as P

B = 64
MODES = 128
BR_DEV = 4
CAP = 128


def shards(basis, springs, tangent_blocks, tile_rows, tile_owner, tile_offset, tile_count):
    row_devices = lax.axis_size("row")
    dof_total = basis.shape[0] * row_devices
    own_blocks = basis.reshape(BR_DEV, B, MODES)
    square_blocks = tangent_blocks.reshape(CAP, B, B)
    owner_ids = tile_owner[:, 0]
    gathered = lax.all_gather(own_blocks, "row", axis=0, tiled=True)
    picked = gathered[owner_ids * BR_DEV + tile_offset]
    live_slot = (jnp.arange(CAP, dtype=jnp.int32) < tile_count[0]).astype(jnp.float32)
    row_ids = jnp.arange(BR_DEV, dtype=jnp.int32)
    products = jnp.einsum("sij,sjk->sik", square_blocks, picked, precision=lax.Precision.HIGHEST)
    row_select = (tile_rows[None, :] == row_ids[:, None]).astype(jnp.float32) * live_slot[None, :]
    summed = jnp.dot(row_select, products.reshape(CAP, B * MODES), precision=lax.Precision.HIGHEST)
    stiff_image = springs[:, None] * basis + summed.reshape(BR_DEV * B, MODES)
    partial_term = (
        jnp.einsum("rm,rn->mn", basis, stiff_image, precision=lax.Precision.HIGHEST) / dof_total
    )
    reduced = lax.psum(partial_term, "row")
    return (stiff_image, reduced)


def solution(mesh):
    in_specs = (
        P(("groups", "row"), None),
        P(("groups", "row")),
        P(("groups", "row"), None),
        P(("groups", "row")),
        P(("groups", "row"), None),
        P(("groups", "row")),
        P(("groups", "row")),
    )
    out_specs = (P(("groups", "row"), None), P("groups", None))
    return jax.shard_map(shards, mesh=mesh, in_specs=in_specs, out_specs=out_specs, check_vma=False)
```

profile of v0, /device:TPU:8, one launch (start us, length us, event | category | flops | bytes accessed | tf_op | source)
XLA Modules:
  0.0 163.7 jit_solution(6896301566178183216)
XLA Ops:
  7.2 0.0 all-gather.2.cloned.1.call-start
  7.2 0.7 all-gather.2.cloned.1.call-update
  7.9 0.0 all-reduce.2.cloned.1.call-start
  7.9 1.9 %copy.13 = f32[128,4096]{0,1:T(8,128)S(1)} copy(f32[128,4096]{1,0:T(8,128)} %param.9) | data formatting | bytes 4194304 | tf_op args[2]
  9.9 0.0 copy-start.4
  9.9 0.0 copy-start.5
  9.9 4.5 %copy.14 = f32[128,64,64]{2,1,0:T(8,128)} copy(f32[128,64,64]{0,2,1:T(8,128)S(1)} %bitcast.20) | data formatting | bytes 4194304 | tf_op jit(solution)/shard_map/reshape | solution.py:16
  15.1 0.0 copy-done.4
  15.1 0.0 copy-done.5
  15.1 36.7 %all-gather.2.cloned.1.call-done = f32[64,64,128]{2,1,0:T(8,128)} async-done(((f32[4,64,128]{2,1,0:T(8,128)}), f32[64,64,128]{2,1,0:T(8,128)}) %all-gather.2.cloned.1.call-update) | async-done | bytes 2097168 | tf_op jit(solution)/shard_map/all_gather | solution.py:18
  51.8 4.4 %gather_fusion = f32[128,64,128]{2,1,0:T(8,128)} fusion(f32[64,64,128]{2,1,0:T(8,128)} %all-gather.2.cloned.1.call-done, s32[1024]{0:T(1024)S(1)} %pad_clamp_fusion), kind=kCustom, calls=%fused_computation | custom fusion | bytes 8389120 | tf_op jit(solution)/shard_map/gather | solution.py:19
  56.1 0.0 copy-start.3
  56.1 6.5 %fusion.9 = f32[128,128,64]{1,2,0:T(8,128)S(1)} fusion(f32[128,64,128]{2,1,0:T(8,128)} %gather_fusion, f32[128,64,64]{2,1,0:T(8,128)} %copy.14), kind=kOutput, calls=%fused_computation.17 | convolution fusion | flops 805306368 | bytes 10485760 | tf_op jit(solution)/shard_map/sij,sjk->sik/dot_general | solution.py:22
  62.7 0.0 copy-start
  62.7 0.0 copy-start.2
  62.7 0.0 copy-done.3
  62.7 4.3 %fusion = f32[4,8192]{1,0:T(4,128)S(1)} fusion(f32[16,8,64,128]{3,2,1,0:T(8,128)S(1)} %bitcast.19, f32[128]{0:T(128)S(1)} %compare_convert_fusion, s32[128]{0:T(128)S(1)} %copy-done.3), kind=kOutput, calls=%fused_computation.1 | convolution fusion | flops 50332672 | bytes 4326400 | tf_op jit(solution)/shard_map/dot_general | solution.py:24
  67.1 0.1 reshape.28
  67.2 0.0 copy-done
  67.2 0.0 copy-done.2
  67.2 0.1 multiply_add_fusion
  67.3 0.0 copy-start.1
  67.3 1.0 fusion.3
  68.3 0.0 all-reduce.2.cloned.1.call-update
  68.3 86.9 %all-reduce.2.cloned.1.call-done = f32[128,128]{0,1:T(8,128)} async-done(((f32[128,128]{0,1:T(8,128)}), f32[128,128]{0,1:T(8,128)}) %all-reduce.2.cloned.1.call-update) | async-done | bytes 65552 | tf_op jit(solution)/shard_map/psum | solution.py:29
  155.3 1.6 copy.15
  156.8 0.0 copy-done.1
  (3 shorter events, 0.0 us)
Async XLA Ops:
  7.2 44.6 %all-gather.2.cloned.1.call-start = ((), (), s32[]{:S(2)}) async-start(), calls=%async_computation | async-start | bytes 2228224 | tf_op jit(solution)/shard_map/all_gather | solution.py:18
  7.9 147.4 %all-reduce.2.cloned.1.call-start = ((), (), s32[]{:S(2)}) async-start(), calls=%async_computation.1 | async-start | bytes 131072 | tf_op jit(solution)/shard_map/psum | solution.py:29
  9.9 5.2 %copy-start.4 = (s32[128]{0:T(128)S(1)}, s32[128]{0:T(128)}, u32[]{:S(2)}) copy-start(s32[128]{0:T(128)} %param.12) | copy-start | bytes 1540
  9.9 5.2 %copy-start.5 = (s32[128,1]{0,1:T(1,128)S(1)}, s32[128,1]{0,1:T(1,128)}, u32[]{:S(2)}) copy-start(s32[128,1]{0,1:T(1,128)} %param.11) | copy-start | bytes 1540
  56.1 6.6 %copy-start.3 = (s32[128]{0:T(128)S(1)}, s32[128]{0:T(128)}, u32[]{:S(2)}) copy-start(s32[128]{0:T(128)} %param.10) | copy-start | bytes 1540
  62.7 4.5 %copy-start = (f32[256,128]{1,0:T(8,128)S(1)}, f32[256,128]{1,0:T(8,128)}, u32[]{:S(2)}) copy-start(f32[256,128]{1,0:T(8,128)} %param.7) | copy-start | bytes 393220
  62.7 4.5 %copy-start.2 = (f32[256]{0:T(256)S(1)}, f32[256]{0:T(256)}, u32[]{:S(2)}) copy-start(f32[256]{0:T(256)} %param.8) | copy-start | bytes 3076
  67.3 89.5 %copy-start.1 = (f32[256,128]{1,0:T(8,128)}, f32[256,128]{1,0:T(8,128)S(1)}, u32[]{:S(2)}) copy-start(f32[256,128]{1,0:T(8,128)S(1)} %multiply_add_fusion) | copy-start | bytes 393220
Sparse Core Ops, SparseCore 0:
  10.2 41.5 all-gather.1
  68.5 86.7 all-reduce.1
where the time goes:
time: 164 us
  waiting for transfers between devices  124 us (76%)
  between operations  14.8 us (9%)
  local copies, waits for them, and re-layouts  12.5 us (8%)
  matrix products  11.9 us (7%)
    psum x1, waiting for transfers between devices, shards(): reduced = lax.psum(partial_term, 'row')  86.9 us
    all_gather x1, waiting for transfers between devices, shards(): gathered = lax.all_gather(own_blocks, 'row', axis=0, tiled=True)  36.7 us
    dot_general x1, matrix products, shards(): jnp.einsum('sij,sjk->sik', square_blocks, picked, precision=lax.Precision...  6.52 us
    reshape x1, local copies, waits for them, and re-layouts, shards(): square_blocks = tangent_blocks.reshape(CAP, B, B)  4.52 us
    gather x1, local copies, waits for them, and re-layouts, shards(): picked = gathered[owner_ids * BR_DEV + tile_offset]  4.35 us
    dot_general x1, matrix products, shards(): jnp.dot(row_select, products.reshape(CAP, B * MODES), precision=lax.Preci...  4.34 us
    unnamed x14, local copies, waits for them, and re-layouts  3.52 us
  transfers between devices with their start and end apart: 2, of which 2 were waited for; matrix products, arithmetic and copies ran while one was open for 4% of the time, Pallas kernels for 0%

commit v1 on v0

--- a/solution.py
+++ b/solution.py
@@ -26,7 +26,7 @@
     partial_term = (
         jnp.einsum("rm,rn->mn", basis, stiff_image, precision=lax.Precision.HIGHEST) / dof_total
     )
-    reduced = lax.psum(partial_term, "row")
+    reduced = jnp.sum(lax.all_gather(partial_term, "row"), axis=0)
     return (stiff_image, reduced)
 
 

time: 164 us -> 116 us (0.71)
  waiting for transfers between devices: 124 us -> 74.1 us
    psum x1 -> x0, waiting for transfers between devices: 86.9 us -> none  [shards(): reduced = lax.psum(partial_term, 'row')]
    all_gather x0 -> x1, waiting for transfers between devices: none -> 36.7 us  [shards(): reduced = jnp.sum(lax.all_gather(partial_term, 'row'), axis=0)]
    unnamed x14 -> x15, local copies, waits for them, and re-layouts: 3.52 us -> 4.09 us
  transfers between devices with their start and end apart: 2 -> 2, of which waited for: 2 -> 2; matrix products, arithmetic and copies ran while one was open for 4% -> 6% of each run, Pallas kernels for 0% -> 0%
where the time goes in v1:
time: 116 us; the launch traced here: 114 us
  waiting for transfers between devices  74.1 us (64%)
  between operations  14.8 us (13%)
  local copies, waits for them, and re-layouts  13.1 us (11%)
  matrix products  11.9 us (10%)
    all_gather x1, waiting for transfers between devices, shards(): reduced = jnp.sum(lax.all_gather(partial_term, 'row'), axis=0)  36.7 us
    all_gather x1, waiting for transfers between devices, shards(): gathered = lax.all_gather(own_blocks, 'row', axis=0, tiled=True)  36.7 us
    dot_general x1, matrix products, shards(): jnp.einsum('sij,sjk->sik', square_blocks, picked, precision=lax.Precision...  6.52 us
    reshape x1, local copies, waits for them, and re-layouts, shards(): square_blocks = tangent_blocks.reshape(CAP, B, B)  4.52 us
    gather x1, local copies, waits for them, and re-layouts, shards(): picked = gathered[owner_ids * BR_DEV + tile_offset]  4.35 us
    dot_general x1, matrix products, shards(): jnp.dot(row_select, products.reshape(CAP, B * MODES), precision=lax.Preci...  4.34 us
    unnamed x15, local copies, waits for them, and re-layouts  4.09 us
  transfers between devices with their start and end apart: 2, of which 2 were waited for; matrix products, arithmetic and copies ran while one was open for 6% of the time, Pallas kernels for 0%

profile of v1, /device:TPU:8, one launch (start us, length us, event | category | flops | bytes accessed | tf_op | source)
XLA Modules:
  0.0 114.2 jit_solution(9847418301706572811)
XLA Ops:
  7.2 0.0 all-gather.4.cloned.1.call-start
  7.2 0.7 all-gather.4.cloned.1.call-update
  7.9 0.0 all-gather.6.cloned.1.call-start
  7.9 1.9 %copy.11 = f32[128,4096]{0,1:T(8,128)S(1)} copy(f32[128,4096]{1,0:T(8,128)} %param.9) | data formatting | bytes 4194304 | tf_op args[2]
  9.9 0.0 copy-start.4
  9.9 0.0 copy-start.5
  9.9 4.5 %copy.12 = f32[128,64,64]{2,1,0:T(8,128)} copy(f32[128,64,64]{0,2,1:T(8,128)S(1)} %bitcast.25) | data formatting | bytes 4194304 | tf_op jit(solution)/shard_map/reshape | solution.py:16
  15.1 0.0 copy-done.4
  15.1 0.0 copy-done.5
  15.1 36.7 %all-gather.4.cloned.1.call-done = f32[64,64,128]{2,1,0:T(8,128)} async-done(((f32[4,64,128]{2,1,0:T(8,128)}), f32[64,64,128]{2,1,0:T(8,128)}) %all-gather.4.cloned.1.call-update) | async-done | bytes 2097168 | tf_op jit(solution)/shard_map/all_gather | solution.py:18
  51.8 4.4 %gather_fusion = f32[128,64,128]{2,1,0:T(8,128)} fusion(f32[64,64,128]{2,1,0:T(8,128)} %all-gather.4.cloned.1.call-done, s32[1024]{0:T(1024)S(1)} %pad_clamp_fusion), kind=kCustom, calls=%fused_computation | custom fusion | bytes 8389120 | tf_op jit(solution)/shard_map/gather | solution.py:19
  56.1 0.0 copy-start.3
  56.1 6.5 %fusion.9 = f32[128,128,64]{1,2,0:T(8,128)S(1)} fusion(f32[128,64,128]{2,1,0:T(8,128)} %gather_fusion, f32[128,64,64]{2,1,0:T(8,128)} %copy.12), kind=kOutput, calls=%fused_computation.18 | convolution fusion | flops 805306368 | bytes 10485760 | tf_op jit(solution)/shard_map/sij,sjk->sik/dot_general | solution.py:22
  62.7 0.0 copy-start
  62.7 0.0 copy-start.2
  62.7 0.0 copy-done.3
  62.7 4.3 %fusion = f32[4,8192]{1,0:T(4,128)S(1)} fusion(f32[16,8,64,128]{3,2,1,0:T(8,128)S(1)} %bitcast.24, f32[128]{0:T(128)S(1)} %compare_convert_fusion, s32[128]{0:T(128)S(1)} %copy-done.3), kind=kOutput, calls=%fused_computation.1 | convolution fusion | flops 50332672 | bytes 4326400 | tf_op jit(solution)/shard_map/dot_general | solution.py:24
  67.1 0.1 reshape.28
  67.2 0.0 copy-done
  67.2 0.0 copy-done.2
  67.2 0.1 multiply_add_fusion
  67.3 0.0 copy-start.1
  67.3 1.0 fusion.3
  68.3 0.0 all-gather.6.cloned.1.call-update
  68.3 36.7 %all-gather.6.cloned.1.call-done = f32[2048,128]{0,1:T(8,128)} async-done(((f32[128,128]{0,1:T(8,128)}), f32[2048,128]{0,1:T(8,128)}) %all-gather.6.cloned.1.call-update) | async-done | bytes 1048592 | tf_op jit(solution)/shard_map/all_gather | solution.py:29
  105.1 1.4 %copy.15 = f32[16,8,16,128]{3,2,1,0:T(8,128)S(1)} copy(f32[16,8,16,128]{3,1,2,0:T(8,128)} %bitcast.27) | data formatting | bytes 2097152
  106.5 0.2 bitcast_reduce_fusion
  106.6 0.7 copy.13
  107.4 0.0 copy-done.1
  (3 shorter events, 0.0 us)
Async XLA Ops:
  7.2 44.6 %all-gather.4.cloned.1.call-start = ((), (), s32[]{:S(2)}) async-start(), calls=%async_computation | async-start | bytes 2228224 | tf_op jit(solution)/shard_map/all_gather | solution.py:18
  7.9 97.2 %all-gather.6.cloned.1.call-start = ((), (), s32[]{:S(2)}) async-start(), calls=%async_computation.1 | async-start | bytes 1114112 | tf_op jit(solution)/shard_map/all_gather | solution.py:29
  9.9 5.2 %copy-start.4 = (s32[128]{0:T(128)S(1)}, s32[128]{0:T(128)}, u32[]{:S(2)}) copy-start(s32[128]{0:T(128)} %param.12) | copy-start | bytes 1540
  9.9 5.2 %copy-start.5 = (s32[128,1]{0,1:T(1,128)S(1)}, s32[128,1]{0,1:T(1,128)}, u32[]{:S(2)}) copy-start(s32[128,1]{0,1:T(1,128)} %param.11) | copy-start | bytes 1540
  56.1 6.6 %copy-start.3 = (s32[128]{0:T(128)S(1)}, s32[128]{0:T(128)}, u32[]{:S(2)}) copy-start(s32[128]{0:T(128)} %param.10) | copy-start | bytes 1540
  62.7 4.5 %copy-start = (f32[256,128]{1,0:T(8,128)S(1)}, f32[256,128]{1,0:T(8,128)}, u32[]{:S(2)}) copy-start(f32[256,128]{1,0:T(8,128)} %param.7) | copy-start | bytes 393220
  62.7 4.5 %copy-start.2 = (f32[256]{0:T(256)S(1)}, f32[256]{0:T(256)}, u32[]{:S(2)}) copy-start(f32[256]{0:T(256)} %param.8) | copy-start | bytes 3076
  67.3 40.1 %copy-start.1 = (f32[256,128]{1,0:T(8,128)}, f32[256,128]{1,0:T(8,128)S(1)}, u32[]{:S(2)}) copy-start(f32[256,128]{1,0:T(8,128)S(1)} %multiply_add_fusion) | copy-start | bytes 393220
Sparse Core Ops, SparseCore 0:
  10.2 41.5 all-gather.3
  68.5 36.5 all-gather.5
